TPU v7x, 128 devices: a whole 4x4x4 slice. The times are simulated.
128 devices in a mesh: inner: 4 (over y_hi, core), outer: 32 (over z, y_lo, x).
Axes of the slice: x: 4, y: 4 (y_hi: 2, y_lo: 2; y = y_hi * 2 + y_lo), z: 4, core: 2. Of those that a mesh axis runs over, the one named last changes fastest.
Arguments:
- gradients: bfloat16 [128, 4096, 1024], P(('inner', 'outer')), may hold values from -400 to 400
- master: float32 [4096, 1024], P(('inner', 'outer')), may hold values from -0.024 to 0.024
- first_moment: float32 [4096, 1024], P(('inner', 'outer')), may hold values from -0.6 to 0.6
- second_moment: float32 [4096, 1024], P(('inner', 'outer')), may hold values from 0.01 to 0.1
Outputs:
- new_master: float32 [4096, 1024], P(('inner', 'outer'))
- new_first: float32 [4096, 1024], P(('inner', 'outer'))
- new_second: float32 [4096, 1024], P(('inner', 'outer'))
- params: bfloat16 [4096, 1024], replicated
All inputs are finite; a program needn't handle non-finite values.
Results may differ from a plain program's by a relative error of at most 0.015.
Values may be sent and summed in bfloat16 or wider, within the bound.
A program may use at most 128 MiB of HBM per device.

v0:
```python
import math

import jax
import jax.numpy as jnp
from jax import lax
from jax.sharding import PartitionSpec as P

code_levels = 127.0
beta_one = 0.9
beta_two = 0.95
learn_rate = 0.002
decay_rate = 0.1
adam_epsilon = 1e-08
first_fix = 1.0 - 0.9**10
second_fix = 1.0 - 0.95**10


def sign_rows(first_row, row_count, block_width):
    row_ids = first_row + lax.broadcasted_iota(jnp.int32, (row_count, block_width), 0)
    col_ids = lax.broadcasted_iota(jnp.int32, (row_count, block_width), 1)
    hashed = (row_ids * block_width + col_ids) * jnp.int32(-1640531535)
    hashed = jnp.bitwise_xor(hashed, jnp.right_shift(hashed, 15))
    hashed = hashed * jnp.int32(-2048144777)
    return 1 - 2 * jnp.bitwise_and(jnp.right_shift(hashed, 13), 1)


def hadamard_table(block_width):
    row_ids = lax.broadcasted_iota(jnp.int32, (block_width, block_width), 0)
    col_ids = lax.broadcasted_iota(jnp.int32, (block_width, block_width), 1)
    common_bits = jnp.bitwise_and(row_ids, col_ids)
    parity = jnp.zeros((block_width, block_width), jnp.int32)
    for bit_pos in range(block_width.bit_length() - 1):
        parity = jnp.bitwise_xor(parity, jnp.bitwise_and(jnp.right_shift(common_bits, bit_pos), 1))
    return (1 - 2 * parity).astype(jnp.float32) / math.sqrt(block_width)


def per_device(gradients, master, first_moment, second_moment):
    gradient_rows = gradients[0]
    blocks, block_width = gradient_rows.shape
    inner_count = lax.axis_size("inner")
    outer_count = lax.axis_size("outer")
    replicas = inner_count * outer_count
    shard = blocks // replicas
    transform = hadamard_table(block_width)
    transform_half = transform.astype(jnp.bfloat16)
    flipped = gradient_rows * sign_rows(0, blocks, block_width).astype(jnp.bfloat16)
    rotated = jnp.dot(flipped, transform_half, preferred_element_type=jnp.float32)
    local_peak = jnp.max(jnp.abs(rotated))
    global_scale = lax.pmax(local_peak, ("inner", "outer"))
    code_ratio = code_levels / (global_scale + 1e-06)
    codes = jnp.floor(rotated * code_ratio + 0.5).astype(jnp.bfloat16)
    partial_value = lax.psum_scatter(
        codes.astype(jnp.float32).astype(jnp.bfloat16), "inner", scatter_dimension=0, tiled=True
    )
    owned_sum = lax.psum_scatter(partial_value, "outer", scatter_dimension=0, tiled=True).astype(
        jnp.float32
    )
    decoded = owned_sum * ((global_scale + 1e-06) / (code_levels * replicas))
    owner = lax.axis_index("inner") * outer_count + lax.axis_index("outer")
    owned_signs = sign_rows(owner * shard, shard, block_width).astype(jnp.float32)
    mean_grad = owned_signs * jnp.dot(decoded, transform, precision=lax.Precision.HIGHEST)
    new_first = beta_one * first_moment + (1.0 - beta_one) * mean_grad
    new_second = beta_two * second_moment + (1.0 - beta_two) * mean_grad * mean_grad
    step_size = new_first / first_fix / (jnp.sqrt(new_second / second_fix) + adam_epsilon)
    new_master = master - learn_rate * (step_size + decay_rate * master)
    param_half = new_master.astype(jnp.bfloat16)
    params = lax.all_gather(param_half, ("inner", "outer"), axis=0, tiled=True)
    return (new_master, new_first, new_second, params)


def solution(mesh):
    in_specs = (
        P(("inner", "outer"), None, None),
        P(("inner", "outer"), None),
        P(("inner", "outer"), None),
        P(("inner", "outer"), None),
    )
    out_specs = (
        P(("inner", "outer"), None),
        P(("inner", "outer"), None),
        P(("inner", "outer"), None),
        P(),
    )
    return jax.shard_map(
        per_device, mesh=mesh, in_specs=in_specs, out_specs=out_specs, check_vma=False
    )
```

profile of v0, /device:TPU:1, one launch (start us, length us, event | category | flops | bytes accessed | tf_op | source)
XLA Modules:
  0.0 685.1 jit_solution(8737446998933939931)
XLA Ops:
  7.2 0.0 reduce-scatter.3.cloned.1.call-start
  7.2 4.8 fusion.17.clone.5
  12.0 21.6 %abs_reduce_fusion = (f32[]{:T(128)}, f32[4096,1024]{1,0:T(8,128)}) fusion(bf16[1,4096,1024]{2,1,0:T(8,128)(2,1)} %param.4, s32[4096]{0:T(1024)S(1)} %iota_multiply_fusion, bf16[1024,1024]{1,0:T(8,128)(2,1)S(1)} %fusion.17.clone.5), kind=kOutput, calls=%fused_computation.8 | convolution fusion | flops 8657043456 | bytes 27279364 | tf_op jit(solution)/shard_map/dot_general | solution.py:47
  33.6 68.7 %pmax.7 = f32[]{:T(128)} all-reduce(f32[]{:T(128)} %get-tuple-element.8), channel_id=1, replica_groups=mesh['inner'=4,'outer'=32] {'inner','outer'}, use_global_device_ids=true, to_apply=%region_1.0 | all-reduce | flops 1 | bytes 8 | tf_op jit(solution)/shard_map/pmax | solution.py:49
  103.0 9.7 %floor_convert_fusion = bf16[4096,1024]{1,0:T(8,128)(2,1)} fusion(f32[4096,1024]{1,0:T(8,128)} %get-tuple-element.9, f32[]{:T(128)S(6)} %div.31), kind=kLoop, calls=%fused_computation.7 | loop fusion | flops 16777216 | bytes 25165828 | tf_op jit(solution)/shard_map/convert_element_type | solution.py:51
  112.7 0.0 copy-start
  112.7 0.0 copy-start.1
  112.7 0.0 copy-start.2
  112.7 0.0 reduce-scatter.3.cloned.1.call-update
  112.7 0.0 reduce-scatter.5.cloned.1.call-start
  112.8 75.2 %reduce-scatter.3.cloned.1.call-done = bf16[1024,1024]{1,0:T(8,128)(2,1)} async-done(((bf16[4096,1024]{1,0:T(8,128)(2,1)}), bf16[1024,1024]{1,0:T(8,128)(2,1)}) %reduce-scatter.3.cloned.1.call-update) | async-done | bytes 2097168 | tf_op jit(solution)/shard_map/reduce_scatter | solution.py:52
  187.9 0.0 reduce-scatter.5.cloned.1.call-update
  187.9 0.0 all-gather.2.cloned.1.call-start
  188.0 140.8 %reduce-scatter.5.cloned.1.call-done = bf16[32,1024]{1,0:T(8,128)(2,1)} async-done(((bf16[1024,1024]{1,0:T(8,128)(2,1)}), bf16[32,1024]{1,0:T(8,128)(2,1)}) %reduce-scatter.5.cloned.1.call-update) | async-done | bytes 65552 | tf_op jit(solution)/shard_map/reduce_scatter | solution.py:55
  328.8 0.0 copy-done
  328.8 0.0 copy-done.1
  328.8 0.0 copy-done.2
  328.8 8.8 %fusion.56 = (bf16[32,1024]{1,0:T(8,128)(2,1)}, f32[32,1024]{1,0:T(8,128)}, f32[32,1024]{1,0:T(8,128)}, f32[32,1024]{1,0:T(8,128)}) fusion(f32[32,1024]{1,0:T(8,128)S(1)} %copy-done, f32[32,1024]{1,0:T(8,128)S(1)} %copy-done.1, f32[32,1024]{1,0:T(8,128)S(1)} %copy-done.2, bf16[32,1024]{1,0:T(8,128)(2,1)} %reduce-scatter.5.cloned.1.call-done, f32[]{:T(128)S(6)} %div.32, ...), kind=kOutput, calls=%fused_computation.65 | convolution fusion | flops 439255040 | bytes 917636 | tf_op jit(solution)/shard_map/dot_general | solution.py:61
  337.6 0.0 all-gather.2.cloned.1.call-update
  337.6 333.2 %all-gather.2.cloned.1.call-done = bf16[4096,1024]{1,0:T(8,128)(2,1)} async-done(((bf16[32,1024]{1,0:T(8,128)(2,1)}), bf16[4096,1024]{1,0:T(8,128)(2,1)}) %all-gather.2.cloned.1.call-update) | async-done | bytes 8388624 | tf_op jit(solution)/shard_map/all_gather | solution.py:67
  670.9 7.8 %copy.9 = bf16[4096,1024]{1,0:T(8,128)(2,1)} copy(bf16[4096,1024]{1,0:T(8,128)(2,1)} %all-gather.2.cloned.1.call-done) | data formatting | bytes 16777216
  (2 shorter events, 0.0 us)
Async XLA Ops:
  7.2 180.8 %reduce-scatter.3.cloned.1.call-start = ((), (), s32[]{:S(2)}) async-start(), calls=%async_computation.2 | async-start | bytes 10485760 | tf_op jit(solution)/shard_map/reduce_scatter | solution.py:52
  112.7 216.1 %copy-start = (f32[32,1024]{1,0:T(8,128)S(1)}, f32[32,1024]{1,0:T(8,128)}, u32[]{:S(2)}) copy-start(f32[32,1024]{1,0:T(8,128)} %param.5) | copy-start | bytes 393220
  112.7 216.1 %copy-start.1 = (f32[32,1024]{1,0:T(8,128)S(1)}, f32[32,1024]{1,0:T(8,128)}, u32[]{:S(2)}) copy-start(f32[32,1024]{1,0:T(8,128)} %param.6) | copy-start | bytes 393220
  112.7 216.1 %copy-start.2 = (f32[32,1024]{1,0:T(8,128)S(1)}, f32[32,1024]{1,0:T(8,128)}, u32[]{:S(2)}) copy-start(f32[32,1024]{1,0:T(8,128)} %param.7) | copy-start | bytes 393220
  112.7 216.1 %reduce-scatter.5.cloned.1.call-start = ((), (), s32[]{:S(2)}) async-start(), calls=%async_computation.3 | async-start | bytes 2162688 | tf_op jit(solution)/shard_map/reduce_scatter | solution.py:55
  187.9 482.9 %all-gather.2.cloned.1.call-start = ((), (), s32[]{:S(2)}) async-start(), calls=%async_computation.4 | async-start | bytes 8454144 | tf_op jit(solution)/shard_map/all_gather | solution.py:67
Sparse Core Ops, SparseCore 0:
  112.8 75.0 reduce-scatter.2
  190.4 138.3 reduce-scatter.4
  337.7 333.0 all-gather.1
where the time goes:
time: 685 us
  waiting for transfers between devices  549 us (80%)
  blocking collectives  68.7 us (10%)
  matrix products  30.4 us (4%)
  other arithmetic  14.5 us (2%)
  between operations  14.5 us (2%)
  local copies, waits for them, and re-layouts  7.77 us (1%)
    all_gather x1, waiting for transfers between devices, per_device(): params = lax.all_gather(param_half, ('inner', 'outer'), axis=0, tiled=True)  333 us
    reduce_scatter x1, waiting for transfers between devices, per_device(): lax.psum_scatter(partial_value, 'outer', scatter_dimension=0, tiled=True)  141 us
    reduce_scatter x1, waiting for transfers between devices, per_device(): lax.psum_scatter(codes.astype(jnp.float32).astype(jnp.bfloat16), 'inner',...  75.2 us
    pmax x1, blocking collectives, per_device(): global_scale = lax.pmax(local_peak, ('inner', 'outer'))  68.7 us
    dot_general x1, matrix products, per_device(): jnp.dot(flipped, transform_half, preferred_element_type=jnp.float32)  21.6 us
  transfers between devices with their start and end apart: 3, of which 3 were waited for; matrix products, arithmetic and copies ran while one was open for 0% of the time, Pallas kernels for 0%

commit v1 on v0

v1 whole, which is shorter than its diff:
```python
import functools
import math

import jax
import jax.numpy as jnp
from jax import lax
from jax.experimental import pallas as pl
from jax.experimental.pallas import tpu as pltpu
from jax.sharding import PartitionSpec as P

MESH = pl.DeviceIdType.MESH

code_levels = 127.0
beta_one = 0.9
beta_two = 0.95
learn_rate = 0.002
decay_rate = 0.1
adam_epsilon = 1e-08
first_fix = 1.0 - 0.9**10
second_fix = 1.0 - 0.95**10

blocks = 4096
width = 1024
group = 256
shard = 32
half = 16
lane = 128
tiles = width // lane
units = 2 * tiles
chunk = 256
chunks = blocks // chunk
sub = 128

hash_one = -1640531535
hash_two = ((-2048144777 << 18) & 0xFFFFFFFF) - (1 << 32 if ((-2048144777 << 18) & 0x80000000) else 0)


def wrap(value):
    value &= 0xFFFFFFFF
    return value - (1 << 32) if value & 0x80000000 else value


RS = (0, 2, 4, 6, 8, 10)
AG = (0, 1, 3, 5, 7, 9)


def negative(hashed):
    mixed = jnp.bitwise_xor(hashed, jnp.right_shift(hashed, 15))
    return mixed * jnp.int32(hash_two) < 0


def butterfly(parts):
    p0, p1, p2, p3 = parts
    a, b, c, d = p0 + p1, p0 - p1, p2 + p3, p2 - p3
    return a + c, b + d, a - c, b - d


def pick(order, v0, v1, v2):
    return jnp.where(order == 0, v0, jnp.where(order == 1, v1, v2))


def row_of(axis, v):
    if isinstance(v, int):
        return pick(axis, v * shard, (v % 2) * 128 + (v // 2) * 2048, v * 256)
    return pick(axis, v * shard, lax.rem(v, 2) * 128 + lax.div(v, 2) * 2048, v * 256)


def kernel(
    grad, master, first, second,
    out, new_master, new_first, new_second,
    rot, base, table, peak, peaks, adam_in, total,
    other, core_in, s1, r1, r2, t1, r3, t2, r4, gath, gath_other,
    grad_sem, adam_sem, peak_send, peak_recv,
    rs_send, rs_core, rs_one, rs_two, rs_three, rs_four,
    ag_send, ag_one, ag_two, ag_near, ag_far, ag_core,
):
    inner, outer = lax.axis_index("inner"), lax.axis_index("outer")
    core = lax.rem(inner, 2)
    x = lax.rem(outer, 4)
    y = lax.div(inner, 2) * 2 + lax.rem(lax.div(outer, 4), 2)
    z = lax.div(outer, 8)

    def device(xx, yy, zz, cc):
        return (lax.div(yy, 2) * 2 + cc, zz * 8 + lax.rem(yy, 2) * 4 + xx)

    def step(v, d):
        return lax.rem(v + d, 4)

    near = {}
    for d in (1, 2, 3):
        near[0, d] = device(step(x, d), y, z, core)
        near[1, d] = device(x, step(y, d), z, core)
        near[2, d] = device(x, y, step(z, d), core)
    twin = device(x, y, z, 1 - core)

    def along(axis, d):
        return tuple(pick(axis, near[0, d][n], near[1, d][n], near[2, d][n]) for n in (0, 1))

    def remote(src, dst, send, recv, target):
        return pltpu.make_async_remote_copy(
            src_ref=src, dst_ref=dst, send_sem=send, recv_sem=recv, device_id=target, device_id_type=MESH
        )

    def drain(ref, sem):
        pltpu.make_async_copy(ref, ref, sem).wait()

    barrier = pltpu.get_barrier_semaphore()
    partners = [twin] + [near[axis, d] for axis in (0, 1, 2) for d in (1, 2, 3)]
    for partner in partners:
        pl.semaphore_signal(barrier, inc=1, device_id=partner, device_id_type=MESH)

    def grad_copy(i):
        rows = pl.ds(pl.multiple_of(i * chunk, chunk), chunk)
        return pltpu.make_async_copy(grad.at[0, rows], out.at[rows], grad_sem.at[i])

    def start_grad(i, carry):
        grad_copy(i).start()
        return carry

    lax.fori_loop(0, chunks, start_grad, 0)
    adam_copies = [
        pltpu.make_async_copy(ref, adam_in.at[n], adam_sem.at[n]) for n, ref in enumerate((master, first, second))
    ]
    for copy in adam_copies:
        copy.start()

    rows_i = lax.broadcasted_iota(jnp.int32, (group, group), 0)
    cols_i = lax.broadcasted_iota(jnp.int32, (group, group), 1)
    common = jnp.bitwise_and(rows_i, cols_i)
    for shift in (4, 2, 1):
        common = jnp.bitwise_xor(common, jnp.right_shift(common, shift))
    parity = jnp.bitwise_and(common, 1)
    table[...] = ((1 - 2 * parity).astype(jnp.float32) / math.sqrt(width)).astype(jnp.bfloat16)
    base[...] = (
        lax.broadcasted_iota(jnp.int32, (sub, group), 0) * jnp.int32(wrap(width * hash_one))
        + lax.broadcasted_iota(jnp.int32, (sub, group), 1) * jnp.int32(hash_one)
    )
    peak[...] = jnp.zeros_like(peak)

    def rotate(i, carry):
        @pl.when(lax.rem(i, chunk // sub) == 0)
        def _():
            grad_copy(lax.div(i, chunk // sub)).wait()

        rows = pl.ds(pl.multiple_of(i * sub, sub), sub)
        pieces = []
        for g in range(width // group):
            offset = i * jnp.int32(wrap(sub * width * hash_one)) + jnp.int32(wrap(g * group * hash_one))
            sign = jnp.where(negative(base[...] + offset), -1.0, 1.0).astype(jnp.bfloat16)
            flipped = out[rows, g * group : (g + 1) * group] * sign
            pieces.append(jnp.dot(flipped, table[...], preferred_element_type=jnp.float32))
        top = peak[...]
        for g, piece in enumerate(butterfly(pieces)):
            rot[rows, g * group : (g + 1) * group] = piece
            top = jnp.maximum(top, jnp.max(jnp.abs(piece).reshape(sub // 8, 8, group), axis=0))
        peak[...] = top
        return carry

    lax.fori_loop(0, blocks // sub, rotate, 0)

    pl.semaphore_wait(barrier, len(partners))
    best = jnp.maximum(peak[:, :lane], peak[:, lane:])
    slot = 0
    stages = [[twin]] + [[near[axis, d] for d in (1, 3, 2)] for axis in (0, 1, 2)]
    for n, stage in enumerate(stages):
        peaks[slot] = best
        sends = []
        for k, target in enumerate(stage):
            copy = remote(peaks.at[slot], peaks.at[slot + 1 + k], peak_send.at[slot + k], peak_recv.at[slot + k], target)
            copy.start()
            sends.append(copy)
        for k, copy in enumerate(sends):
            copy.wait_recv()
            best = jnp.maximum(best, peaks[slot + 1 + k])
        for copy in sends:
            copy.wait_send()
        slot += 1 + len(stage)
    scale = jnp.max(best)
    ratio = code_levels / (scale + 1e-06)
    decode = (scale + 1e-06) / (code_levels * 128)

    def quantise(row, column):
        value = rot[pl.ds(pl.multiple_of(row, half), half), pl.ds(column, lane)]
        return jnp.floor(value * ratio + 0.5)

    def place(u, owner):
        order = lax.rem(u + owner, 3)
        first_row = owner * 1024 + lax.div(u, tiles) * half
        return order, first_row, pl.multiple_of(lax.rem(u, tiles) * lane, lane)

    def axes_of(order):
        a, b, c = order, lax.rem(order + 1, 3), lax.rem(order + 2, 3)
        return a, b, c, pick(a, x, y, z), pick(b, x, y, z), pick(c, x, y, z)

    def each_tile(order, first_row, work):
        a, b, c = order, lax.rem(order + 1, 3), lax.rem(order + 2, 3)
        in_b = [row_of(b, j) for j in range(4)]
        in_c = [row_of(c, k) for k in range(4)]

        def body(i, carry):
            start = first_row + row_of(a, i)
            for j in range(4):
                for k in range(4):
                    work(i, j, k, start + in_b[j] + in_c[k])
            return carry

        lax.fori_loop(0, 4, body, 0)

    def rs0(u):
        order, first_row, column = place(u, 1 - core)

        def work(i, j, k, row):
            other[u, i, j, k] = quantise(row, column).astype(jnp.bfloat16)

        each_tile(order, first_row, work)
        remote(other.at[u], core_in.at[u], rs_send.at[0], rs_core.at[u], twin).start()

    def rs1(u):
        order, first_row, column = place(u, core)
        drain(core_in.at[u], rs_core.at[u])

        def work(i, j, k, row):
            mine = quantise(row, column)
            s1[u, i, j, k] = (mine + core_in[u, i, j, k].astype(jnp.float32)).astype(jnp.bfloat16)

        each_tile(order, first_row, work)
        a, _, _, pa, _, _ = axes_of(order)
        up, down = along(a, 1), along(a, 3)
        far, pu, pd = step(pa, 2), step(pa, 1), step(pa, 3)
        lo, hi = pl.ds(0, 2), pl.ds(2, 2)
        remote(s1.at[u, far, lo], r1.at[u, 0], rs_send.at[1], rs_one.at[u], up).start()
        remote(s1.at[u, far, hi], r1.at[u, 1], rs_send.at[1], rs_one.at[u], down).start()
        remote(s1.at[u, pu, hi], r2.at[u, 0, hi], rs_send.at[1], rs_two.at[u], up).start()
        remote(s1.at[u, pd, lo], r2.at[u, 1, lo], rs_send.at[1], rs_two.at[u], down).start()

    def rs2(u):
        order, _, _ = place(u, core)
        a, _, _, pa, _, _ = axes_of(order)
        pu, pd = step(pa, 1), step(pa, 3)
        lo, hi = pl.ds(0, 2), pl.ds(2, 2)
        drain(r1.at[u], rs_one.at[u])
        f32 = jnp.float32
        s1[u, pu, lo] = (s1[u, pu, lo].astype(f32) + r1[u, 0].astype(f32)).astype(jnp.bfloat16)
        s1[u, pd, hi] = (s1[u, pd, hi].astype(f32) + r1[u, 1].astype(f32)).astype(jnp.bfloat16)
        remote(s1.at[u, pu, lo], r2.at[u, 0, lo], rs_send.at[2], rs_two.at[u], along(a, 1)).start()
        remote(s1.at[u, pd, hi], r2.at[u, 1, hi], rs_send.at[2], rs_two.at[u], along(a, 3)).start()

    def rs3(u):
        order, _, _ = place(u, core)
        _, b, _, pa, pb, _ = axes_of(order)
        drain(r2.at[u], rs_two.at[u])
        f32 = jnp.float32
        t1[u] = (s1[u, pa].astype(f32) + r2[u, 0].astype(f32) + r2[u, 1].astype(f32)).astype(jnp.bfloat16)
        for n, d in enumerate((1, 3, 2)):
            remote(t1.at[u, step(pb, d)], r3.at[u, n], rs_send.at[3], rs_three.at[u], along(b, d)).start()

    def rs4(u):
        order, _, _ = place(u, core)
        _, _, c, _, pb, pc = axes_of(order)
        drain(r3.at[u], rs_three.at[u])
        f32 = jnp.float32
        t2[u] = (
            t1[u, pb].astype(f32) + r3[u, 0].astype(f32) + r3[u, 1].astype(f32) + r3[u, 2].astype(f32)
        ).astype(jnp.bfloat16)
        for n, d in enumerate((1, 3, 2)):
            remote(t2.at[u, step(pc, d)], r4.at[u, n], rs_send.at[4], rs_four.at[u], along(c, d)).start()

    def rs5(u):
        order, _, column = place(u, core)
        pc = axes_of(order)[5]
        drain(r4.at[u], rs_four.at[u])
        f32 = jnp.float32
        value = t2[u, pc].astype(f32) + r4[u, 0].astype(f32) + r4[u, 1].astype(f32) + r4[u, 2].astype(f32)
        total[pl.ds(pl.multiple_of(lax.div(u, tiles) * half, half), half), pl.ds(column, lane)] = value

        @pl.when(lax.rem(u, tiles) == tiles - 1)
        def _():
            update(lax.div(u, tiles))

    owner = inner * 32 + outer

    def update(h):
        rows = pl.ds(pl.multiple_of(h * half, half), half)
        lows, highs = [], []
        for g in range(width // group):
            value = total[rows, g * group : (g + 1) * group]
            high = jnp.floor(value * (1.0 / 128.0) + 0.5)
            highs.append(high.astype(jnp.bfloat16))
            lows.append((value - high * 128.0).astype(jnp.bfloat16))
        stacked = jnp.concatenate(highs + lows, axis=0)
        product = jnp.dot(stacked, table[...], preferred_element_type=jnp.float32)
        parts = []
        for g in range(width // group):
            parts.append(
                product[g * half : (g + 1) * half] * 128.0 + product[(g + 4) * half : (g + 5) * half]
            )
        for g, turned in enumerate(butterfly(parts)):
            columns = slice(g * group, (g + 1) * group)
            offset = (owner * shard + h * half) * jnp.int32(wrap(width * hash_one)) + jnp.int32(wrap(g * group * hash_one))
            mean = turned * decode
            mean = jnp.where(negative(base[:half] + offset), -mean, mean)
            one = beta_one * adam_in[1, rows, columns] + (1.0 - beta_one) * mean
            two = beta_two * adam_in[2, rows, columns] + (1.0 - beta_two) * mean * mean
            old = adam_in[0, rows, columns]
            size = one / first_fix / (jnp.sqrt(two / second_fix) + adam_epsilon)
            new = old - learn_rate * (size + decay_rate * old)
            new_first[rows, columns] = one
            new_second[rows, columns] = two
            new_master[rows, columns] = new
            param = new.astype(jnp.bfloat16)
            for n in range(group // lane):
                u = h * tiles + g * (group // lane) + n
                order, _, _ = place(u, core)
                _, _, c, pa, pb, pc = axes_of(order)
                gath[u, pa, pb, pc] = param[:, n * lane : (n + 1) * lane]
                for d in (1, 3, 2):
                    remote(gath.at[u, pa, pb, pc], gath.at[u, pa, pb, pc], ag_send.at[0], ag_one.at[u], along(c, d)).start()

    def ag1(u):
        order, _, _ = place(u, core)
        _, b, _, pa, pb, _ = axes_of(order)
        drain(r4.at[u], ag_one.at[u])
        for d in (1, 3, 2):
            remote(gath.at[u, pa, pb], gath.at[u, pa, pb], ag_send.at[1], ag_two.at[u], along(b, d)).start()

    def ag2(u):
        order, _, _ = place(u, core)
        a, _, _, pa, _, _ = axes_of(order)
        drain(r3.at[u], ag_two.at[u])
        up, down = along(a, 1), along(a, 3)
        lo, hi = gath.at[u, pa, pl.ds(0, 2)], gath.at[u, pa, pl.ds(2, 2)]
        remote(lo, lo, ag_send.at[2], ag_near.at[u], up).start()
        remote(hi, hi, ag_send.at[2], ag_near.at[u], down).start()
        remote(hi, hi, ag_send.at[2], ag_far.at[u], up).start()
        remote(lo, lo, ag_send.at[2], ag_far.at[u], down).start()

    def ag3(u):
        order, _, _ = place(u, core)
        a, _, _, pa, _, _ = axes_of(order)
        drain(r1.at[u], ag_near.at[u])
        lo, hi = gath.at[u, step(pa, 3), pl.ds(0, 2)], gath.at[u, step(pa, 1), pl.ds(2, 2)]
        remote(lo, lo, ag_send.at[3], ag_far.at[u], along(a, 1)).start()
        remote(hi, hi, ag_send.at[3], ag_far.at[u], along(a, 3)).start()

    def lay_out(u, source, from_core):
        order, first_row, column = place(u, from_core)

        def work(i, j, k, row):
            out[pl.ds(pl.multiple_of(row, half), half), pl.ds(column, lane)] = source[u, i, j, k]

        each_tile(order, first_row, work)

    def ag4(u):
        drain(r2.at[u], ag_far.at[u])
        remote(gath.at[u], gath_other.at[u], ag_send.at[4], ag_core.at[u], twin).start()
        lay_out(u, gath, core)

    def ag5(u):
        drain(gath_other.at[u], ag_core.at[u])
        lay_out(u, gath_other, 1 - core)

    for copy in adam_copies:
        copy.wait()
    lead = tiles - 1 + RS[5]
    plan = [(ag5, lead + AG[5]), (ag4, lead + AG[4]), (ag3, lead + AG[3]), (ag2, lead + AG[2]), (ag1, lead + AG[1])]
    plan += [(rs5, RS[5]), (rs4, RS[4]), (rs3, RS[3]), (rs2, RS[2]), (rs1, RS[1]), (rs0, RS[0])]

    def tick(t, carry):
        for work, delay in plan:
            @pl.when(jnp.logical_and(t >= delay, t < delay + units))
            def _(work=work, delay=delay):
                work(t - delay)
        return carry

    lax.fori_loop(0, units + lead + AG[5], tick, 0)

    drain(other, rs_send.at[0])
    drain(r2, rs_send.at[1])
    drain(r1, rs_send.at[2])
    drain(r3, rs_send.at[3])
    drain(r4, rs_send.at[4])
    drain(r4, ag_send.at[0])
    drain(r3, ag_send.at[1])
    drain(r2, ag_send.at[2])
    drain(r1, ag_send.at[3])
    drain(gath, ag_send.at[4])


def per_device(gradients, master, first_moment, second_moment):
    bf16, f32 = jnp.bfloat16, jnp.float32
    anywhere = pl.BlockSpec(memory_space=pl.ANY)
    in_vmem = pl.BlockSpec(memory_space=pltpu.VMEM)
    piece = (4, half, lane)
    dma = pltpu.SemaphoreType.DMA
    params, new_master, new_first, new_second = pl.pallas_call(
        kernel,
        out_shape=(
            pltpu.VMEM((blocks, width), bf16),
            pltpu.VMEM((shard, width), f32),
            pltpu.VMEM((shard, width), f32),
            pltpu.VMEM((shard, width), f32),
        ),
        in_specs=[anywhere] * 4,
        out_specs=(in_vmem,) * 4,
        scratch_shapes=[
            pltpu.VMEM((blocks, width), f32),
            pltpu.VMEM((sub, group), jnp.int32),
            pltpu.VMEM((group, group), bf16),
            pltpu.VMEM((8, group), f32),
            pltpu.VMEM((14, 8, lane), f32),
            pltpu.VMEM((3, shard, width), f32),
            pltpu.VMEM((shard, width), f32),
            pltpu.VMEM((units, 4, 4) + piece, bf16),
            pltpu.VMEM((units, 4, 4) + piece, bf16),
            pltpu.VMEM((units, 4, 4) + piece, bf16),
            pltpu.VMEM((units, 2, 2) + piece, bf16),
            pltpu.VMEM((units, 2, 4) + piece, bf16),
            pltpu.VMEM((units, 4) + piece, bf16),
            pltpu.VMEM((units, 3) + piece, bf16),
            pltpu.VMEM((units,) + piece, bf16),
            pltpu.VMEM((units, 3, half, lane), bf16),
            pltpu.VMEM((units, 4, 4) + piece, bf16),
            pltpu.VMEM((units, 4, 4) + piece, bf16),
            dma((chunks,)), dma((3,)), dma((14,)), dma((14,)),
            dma((5,)), dma((units,)), dma((units,)), dma((units,)), dma((units,)), dma((units,)),
            dma((5,)), dma((units,)), dma((units,)), dma((units,)), dma((units,)), dma((units,)),
        ],
        compiler_params=pltpu.CompilerParams(
            collective_id=0, has_side_effects=True, vmem_limit_bytes=50 * 2**20
        ),
        cost_estimate=pl.CostEstimate(flops=2 * 2**32, bytes_accessed=2**25, transcendentals=0),
        name="reduce_step",
    )(gradients, master, first_moment, second_moment)
    return (new_master, new_first, new_second, params)


def solution(mesh):
    in_specs = (
        P(("inner", "outer"), None, None),
        P(("inner", "outer"), None),
        P(("inner", "outer"), None),
        P(("inner", "outer"), None),
    )
    out_specs = (
        P(("inner", "outer"), None),
        P(("inner", "outer"), None),
        P(("inner", "outer"), None),
        P(),
    )
    return jax.shard_map(
        per_device, mesh=mesh, in_specs=in_specs, out_specs=out_specs, check_vma=False
    )
```

time: 685 us -> 117 us (0.17)
  waiting for transfers between devices: 549 us -> 0 us
  Pallas kernels: 0 us -> 111 us
  blocking collectives: 68.7 us -> 0 us
  matrix products: 30.4 us -> 0 us
  other arithmetic: 14.5 us -> 0 us
  between operations: 14.5 us -> 0.64 us
    all_gather x1 -> x0, waiting for transfers between devices: 333 us -> none  [per_device(): params = lax.all_gather(param_half, ('inner', 'outer'), axis=0, tiled=True)]
    reduce_scatter x2 -> x0, waiting for transfers between devices: 216 us -> none  [the longest x1 141 us: per_device(): lax.psum_scatter(partial_value, 'outer', scatter_dimension=0, tiled=True)]
    pallas_call x0 -> x1, Pallas kernels: none -> 111 us  [per_device(): pl.pallas_call(kernel, out_shape=(pltpu.VMEM((blocks, width), bf16), pltp...]
    pmax x1 -> x0, blocking collectives: 68.7 us -> none  [per_device(): global_scale = lax.pmax(local_peak, ('inner', 'outer'))]
    dot_general x2 -> x0, matrix products: 30.4 us -> none  [the longest x1 21.6 us: per_device(): jnp.dot(flipped, transform_half, preferred_element_type=jnp.float32)]
    convert_element_type x1 -> x0, other arithmetic: 9.68 us -> none  [per_device(): codes = jnp.floor(rotated * code_ratio + 0.5).astype(jnp.bfloat16)]
  transfers between devices with their start and end apart: 3 -> 0, of which waited for: 3 -> 0; matrix products, arithmetic and copies ran while one was open for 0% -> 0% of each run, Pallas kernels for 0% -> 0%
where the time goes in v1:
time: 117 us
  Pallas kernels  111 us (95%)
  local copies, waits for them, and re-layouts  5.36 us (5%)
    pallas_call x1, Pallas kernels, per_device(): pl.pallas_call(kernel, out_shape=(pltpu.VMEM((blocks, width), bf16), pltp...  111 us
    unnamed x4, local copies, waits for them, and re-layouts  5.36 us

profile of v1, /device:TPU:1, one launch (start us, length us, event | category | flops | bytes accessed | tf_op | source)
XLA Modules:
  0.0 116.6 jit_solution(3739163858521273712)
XLA Ops:
  0.6 110.5 %reduce_step.1 = (bf16[4096,1024]{1,0:T(8,128)(2,1)S(1)}, f32[32,1024]{1,0:T(8,128)S(1)}, f32[32,1024]{1,0:T(8,128)S(1)}, f32[32,1024]{1,0:T(8,128)S(1)}) custom-call(bf16[1,4096,1024]{2,1,0:T(8,128)(2,1)} %grad.1, f32[32,1024]{1,0:T(8,128)} %master.1, f32[32,1024]{1,0:T(8,128)} %first.1, f32[32,1024]{1,0:T(8,128)} %second.1), custom_call_target="tpu_custom_call" | custom-call | flops 8589934592 | bytes 33554432 | tf_op jit(solution)/shard_map/reduce_step/pallas_call | solution.py:395
  111.2 0.7 copy.12
  111.8 0.7 copy.13
  112.5 0.7 copy.14
  113.2 3.4 %copy.15 = bf16[4096,1024]{1,0:T(8,128)(2,1)} copy(bf16[4096,1024]{1,0:T(8,128)(2,1)S(1)} %get-tuple-element.15) | data formatting | bytes 16777216

commit v2 on v1

--- a/solution.py
+++ b/solution.py
@@ -27,9 +27,9 @@
 lane = 128
 tiles = width // lane
 units = 2 * tiles
-chunk = 256
+chunk = 512
 chunks = blocks // chunk
-sub = 128
+sub = 512
 
 hash_one = -1640531535
 hash_two = ((-2048144777 << 18) & 0xFFFFFFFF) - (1 << 32 if ((-2048144777 << 18) & 0x80000000) else 0)
@@ -40,8 +40,8 @@
     return value - (1 << 32) if value & 0x80000000 else value
 
 
-RS = (0, 2, 4, 6, 8, 10)
-AG = (0, 1, 3, 5, 7, 9)
+RS = (0, 8, 13, 17, 23, 29)
+AG = (0, 3, 9, 13, 18, 21)
 
 
 def negative(hashed):
@@ -67,8 +67,8 @@
 
 def kernel(
     grad, master, first, second,
-    out, new_master, new_first, new_second,
-    rot, base, table, peak, peaks, adam_in, total,
+    out, fresh,
+    rot, base, table, peak, peaks_one, peaks_two, adam_in, total,
     other, core_in, s1, r1, r2, t1, r3, t2, r4, gath, gath_other,
     grad_sem, adam_sem, peak_send, peak_recv,
     rs_send, rs_core, rs_one, rs_two, rs_three, rs_four,
@@ -105,7 +105,9 @@
         pltpu.make_async_copy(ref, ref, sem).wait()
 
     barrier = pltpu.get_barrier_semaphore()
-    partners = [twin] + [near[axis, d] for axis in (0, 1, 2) for d in (1, 2, 3)]
+    column = [device(x, y, step(z, d), c) for d in range(4) for c in (core, 1 - core)][1:]
+    plane = [device(step(x, d), step(y, e), z, core) for d in range(4) for e in range(4)][1:]
+    partners = column + plane
     for partner in partners:
         pl.semaphore_signal(barrier, inc=1, device_id=partner, device_id_type=MESH)
 
@@ -138,17 +140,16 @@
     peak[...] = jnp.zeros_like(peak)
 
     def rotate(i, carry):
-        @pl.when(lax.rem(i, chunk // sub) == 0)
-        def _():
-            grad_copy(lax.div(i, chunk // sub)).wait()
-
+        grad_copy(i).wait()
         rows = pl.ds(pl.multiple_of(i * sub, sub), sub)
         pieces = []
         for g in range(width // group):
             offset = i * jnp.int32(wrap(sub * width * hash_one)) + jnp.int32(wrap(g * group * hash_one))
             sign = jnp.where(negative(base[...] + offset), -1.0, 1.0).astype(jnp.bfloat16)
             flipped = out[rows, g * group : (g + 1) * group] * sign
-            pieces.append(jnp.dot(flipped, table[...], preferred_element_type=jnp.float32))
+            pieces.append(flipped)
+        turned = jnp.dot(jnp.concatenate(pieces, axis=0), table[...], preferred_element_type=jnp.float32)
+        pieces = [turned[g * sub : (g + 1) * sub] for g in range(width // group)]
         top = peak[...]
         for g, piece in enumerate(butterfly(pieces)):
             rot[rows, g * group : (g + 1) * group] = piece
@@ -159,22 +160,15 @@
     lax.fori_loop(0, blocks // sub, rotate, 0)
 
     pl.semaphore_wait(barrier, len(partners))
-    best = jnp.maximum(peak[:, :lane], peak[:, lane:])
-    slot = 0
-    stages = [[twin]] + [[near[axis, d] for d in (1, 3, 2)] for axis in (0, 1, 2)]
-    for n, stage in enumerate(stages):
-        peaks[slot] = best
-        sends = []
+    best = jnp.max(jnp.maximum(peak[:, :lane], peak[:, lane:]), axis=0, keepdims=True)
+    for n, (stage, box) in enumerate(((column, peaks_one), (plane, peaks_two))):
+        box[0, :1] = best
         for k, target in enumerate(stage):
-            copy = remote(peaks.at[slot], peaks.at[slot + 1 + k], peak_send.at[slot + k], peak_recv.at[slot + k], target)
-            copy.start()
-            sends.append(copy)
-        for k, copy in enumerate(sends):
-            copy.wait_recv()
-            best = jnp.maximum(best, peaks[slot + 1 + k])
-        for copy in sends:
-            copy.wait_send()
-        slot += 1 + len(stage)
+            remote(box.at[0, :1], box.at[1 + k, :1], peak_send.at[n], peak_recv.at[n], target).start()
+        arrived = box.at[pl.ds(1, len(stage)), :1]
+        drain(arrived, peak_recv.at[n])
+        for k in range(len(stage)):
+            best = jnp.maximum(best, box[1 + k, :1])
     scale = jnp.max(best)
     ratio = code_levels / (scale + 1e-06)
     decode = (scale + 1e-06) / (code_levels * 128)
@@ -304,9 +298,9 @@
             old = adam_in[0, rows, columns]
             size = one / first_fix / (jnp.sqrt(two / second_fix) + adam_epsilon)
             new = old - learn_rate * (size + decay_rate * old)
-            new_first[rows, columns] = one
-            new_second[rows, columns] = two
-            new_master[rows, columns] = new
+            fresh[1, rows, columns] = one
+            fresh[2, rows, columns] = two
+            fresh[0, rows, columns] = new
             param = new.astype(jnp.bfloat16)
             for n in range(group // lane):
                 u = h * tiles + g * (group // lane) + n
@@ -365,6 +359,8 @@
     plan = [(ag5, lead + AG[5]), (ag4, lead + AG[4]), (ag3, lead + AG[3]), (ag2, lead + AG[2]), (ag1, lead + AG[1])]
     plan += [(rs5, RS[5]), (rs4, RS[4]), (rs3, RS[3]), (rs2, RS[2]), (rs1, RS[1]), (rs0, RS[0])]
 
+    plan = plan[::-1]
+
     def tick(t, carry):
         for work, delay in plan:
             @pl.when(jnp.logical_and(t >= delay, t < delay + units))
@@ -374,6 +370,8 @@
 
     lax.fori_loop(0, units + lead + AG[5], tick, 0)
 
+    for n, box in enumerate((peaks_one, peaks_two)):
+        drain(box.at[pl.ds(1, (7, 15)[n]), :1], peak_send.at[n])
     drain(other, rs_send.at[0])
     drain(r2, rs_send.at[1])
     drain(r1, rs_send.at[2])
@@ -392,22 +390,21 @@
     in_vmem = pl.BlockSpec(memory_space=pltpu.VMEM)
     piece = (4, half, lane)
     dma = pltpu.SemaphoreType.DMA
-    params, new_master, new_first, new_second = pl.pallas_call(
+    params, fresh = pl.pallas_call(
         kernel,
         out_shape=(
             pltpu.VMEM((blocks, width), bf16),
-            pltpu.VMEM((shard, width), f32),
-            pltpu.VMEM((shard, width), f32),
-            pltpu.VMEM((shard, width), f32),
+            pltpu.VMEM((3, shard, width), f32),
         ),
         in_specs=[anywhere] * 4,
-        out_specs=(in_vmem,) * 4,
+        out_specs=(in_vmem,) * 2,
         scratch_shapes=[
             pltpu.VMEM((blocks, width), f32),
             pltpu.VMEM((sub, group), jnp.int32),
             pltpu.VMEM((group, group), bf16),
             pltpu.VMEM((8, group), f32),
-            pltpu.VMEM((14, 8, lane), f32),
+            pltpu.VMEM((8, 8, lane), f32),
+            pltpu.VMEM((16, 8, lane), f32),
             pltpu.VMEM((3, shard, width), f32),
             pltpu.VMEM((shard, width), f32),
             pltpu.VMEM((units, 4, 4) + piece, bf16),
@@ -421,7 +418,7 @@
             pltpu.VMEM((units, 3, half, lane), bf16),
             pltpu.VMEM((units, 4, 4) + piece, bf16),
             pltpu.VMEM((units, 4, 4) + piece, bf16),
-            dma((chunks,)), dma((3,)), dma((14,)), dma((14,)),
+            dma((chunks,)), dma((3,)), dma((2,)), dma((2,)),
             dma((5,)), dma((units,)), dma((units,)), dma((units,)), dma((units,)), dma((units,)),
             dma((5,)), dma((units,)), dma((units,)), dma((units,)), dma((units,)), dma((units,)),
         ],
@@ -431,7 +428,7 @@
         cost_estimate=pl.CostEstimate(flops=2 * 2**32, bytes_accessed=2**25, transcendentals=0),
         name="reduce_step",
     )(gradients, master, first_moment, second_moment)
-    return (new_master, new_first, new_second, params)
+    return (fresh[0], fresh[1], fresh[2], params)
 
 
 def solution(mesh):

time: 117 us -> 81.2 us (0.69)
  Pallas kernels: 111 us -> 76.3 us
  local copies, waits for them, and re-layouts: 5.36 us -> 4.15 us
    pallas_call x1, Pallas kernels: 111 us -> 76.3 us  [per_device(): pl.pallas_call(kernel, out_shape=(pltpu.VMEM((blocks, width), bf16), pltp...]
    unnamed x4 -> x1, local copies, waits for them, and re-layouts: 5.36 us -> 3.4 us
where the time goes in v2:
time: 81.2 us; the launch traced here: 81.1 us
  Pallas kernels  76.3 us (94%)
  local copies, waits for them, and re-layouts  4.15 us (5%)
    pallas_call x1, Pallas kernels, per_device(): pl.pallas_call(kernel, out_shape=(pltpu.VMEM((blocks, width), bf16), pltp...  76.3 us
    unnamed x1, local copies, waits for them, and re-layouts  3.4 us

profile of v2, /device:TPU:1, one launch (start us, length us, event | category | flops | bytes accessed | tf_op | source)
XLA Modules:
  0.0 81.1 jit_solution(13059026223986353821)
XLA Ops:
  0.6 76.3 %reduce_step.1 = (bf16[4096,1024]{1,0:T(8,128)(2,1)S(1)}, f32[3,32,1024]{2,1,0:T(8,128)S(1)}) custom-call(bf16[1,4096,1024]{2,1,0:T(8,128)(2,1)} %grad.1, f32[32,1024]{1,0:T(8,128)} %master.1, f32[32,1024]{1,0:T(8,128)} %first.1, f32[32,1024]{1,0:T(8,128)} %second.1), custom_call_target="tpu_custom_call" | custom-call | flops 8589934592 | bytes 33554432 | tf_op jit(solution)/shard_map/reduce_step/pallas_call | solution.py:393
  76.9 0.8 slice_bitcast_fusion
  77.7 3.4 %copy.9 = bf16[4096,1024]{1,0:T(8,128)(2,1)} copy(bf16[4096,1024]{1,0:T(8,128)(2,1)S(1)} %get-tuple-element.14) | data formatting | bytes 16777216

commit v3 on v2

--- a/solution.py
+++ b/solution.py
@@ -3,6 +3,7 @@
 
 import jax
 import jax.numpy as jnp
+import numpy as np
 from jax import lax
 from jax.experimental import pallas as pl
 from jax.experimental.pallas import tpu as pltpu
@@ -25,8 +26,10 @@
 shard = 32
 half = 16
 lane = 128
-tiles = width // lane
-units = 2 * tiles
+rows_of = 8
+wide = 2 * lane
+tiles = width // wide
+units = shard // rows_of * tiles
 chunk = 512
 chunks = blocks // chunk
 sub = 512
@@ -40,8 +43,16 @@
     return value - (1 << 32) if value & 0x80000000 else value
 
 
-RS = (0, 8, 13, 17, 23, 29)
-AG = (0, 3, 9, 13, 18, 21)
+RS = (0, 9, 14, 18, 24, 30)
+AG = (0, 4, 10, 15, 20, 23)
+
+
+def sign_words():
+    at = np.arange(blocks * width, dtype=np.uint32).reshape(blocks, width)
+    hashed = (at * np.uint32(hash_one & 0xFFFFFFFF)).view(np.int32)
+    hashed = np.bitwise_xor(hashed, np.right_shift(hashed, 15)).view(np.uint32) * np.uint32(-2048144777 & 0xFFFFFFFF)
+    bits = ((hashed >> np.uint32(13)) & np.uint32(1)).reshape(blocks // 256, 32, 8, width)
+    return (bits << np.arange(32, dtype=np.uint32)[None, :, None, None]).sum(axis=1, dtype=np.uint32).view(np.int32)
 
 
 def negative(hashed):
@@ -66,11 +77,11 @@
 
 
 def kernel(
-    grad, master, first, second,
+    grad, master, first, second, words,
     out, fresh,
-    rot, base, table, peak, peaks_one, peaks_two, adam_in, total,
+    rot, base, signs, table, peak, peaks_one, peaks_two, adam_in, total,
     other, core_in, s1, r1, r2, t1, r3, t2, r4, gath, gath_other,
-    grad_sem, adam_sem, peak_send, peak_recv,
+    grad_sem, sign_sem, adam_sem, peak_send, peak_recv,
     rs_send, rs_core, rs_one, rs_two, rs_three, rs_four,
     ag_send, ag_one, ag_two, ag_near, ag_far, ag_core,
 ):
@@ -119,6 +130,8 @@
         grad_copy(i).start()
         return carry
 
+    sign_copy = pltpu.make_async_copy(words, signs, sign_sem.at[0])
+    sign_copy.start()
     lax.fori_loop(0, chunks, start_grad, 0)
     adam_copies = [
         pltpu.make_async_copy(ref, adam_in.at[n], adam_sem.at[n]) for n, ref in enumerate((master, first, second))
@@ -134,18 +147,21 @@
     parity = jnp.bitwise_and(common, 1)
     table[...] = ((1 - 2 * parity).astype(jnp.float32) / math.sqrt(width)).astype(jnp.bfloat16)
     base[...] = (
-        lax.broadcasted_iota(jnp.int32, (sub, group), 0) * jnp.int32(wrap(width * hash_one))
-        + lax.broadcasted_iota(jnp.int32, (sub, group), 1) * jnp.int32(hash_one)
+        lax.broadcasted_iota(jnp.int32, (rows_of, group), 0) * jnp.int32(wrap(width * hash_one))
+        + lax.broadcasted_iota(jnp.int32, (rows_of, group), 1) * jnp.int32(hash_one)
     )
     peak[...] = jnp.zeros_like(peak)
+
+    sign_copy.wait()
 
     def rotate(i, carry):
         grad_copy(i).wait()
         rows = pl.ds(pl.multiple_of(i * sub, sub), sub)
         pieces = []
         for g in range(width // group):
-            offset = i * jnp.int32(wrap(sub * width * hash_one)) + jnp.int32(wrap(g * group * hash_one))
-            sign = jnp.where(negative(base[...] + offset), -1.0, 1.0).astype(jnp.bfloat16)
+            held = [signs[i * (sub // 256) + n, :, g * group : (g + 1) * group] for n in range(sub // 256)]
+            shifted = [jnp.left_shift(word, 31 - r) for word in held for r in range(32)]
+            sign = jnp.where(jnp.concatenate(shifted, axis=0) < 0, -1.0, 1.0).astype(jnp.bfloat16)
             flipped = out[rows, g * group : (g + 1) * group] * sign
             pieces.append(flipped)
         turned = jnp.dot(jnp.concatenate(pieces, axis=0), table[...], preferred_element_type=jnp.float32)
@@ -173,14 +189,17 @@
     ratio = code_levels / (scale + 1e-06)
     decode = (scale + 1e-06) / (code_levels * 128)
 
+    def fold(value):
+        return jnp.concatenate([value[:, :lane], value[:, lane:]], axis=0)
+
     def quantise(row, column):
-        value = rot[pl.ds(pl.multiple_of(row, half), half), pl.ds(column, lane)]
-        return jnp.floor(value * ratio + 0.5)
+        value = rot[pl.ds(pl.multiple_of(row, rows_of), rows_of), pl.ds(column, wide)]
+        return fold(jnp.floor(value * ratio + 0.5))
 
     def place(u, owner):
         order = lax.rem(u + owner, 3)
-        first_row = owner * 1024 + lax.div(u, tiles) * half
-        return order, first_row, pl.multiple_of(lax.rem(u, tiles) * lane, lane)
+        first_row = owner * 1024 + lax.div(u, tiles) * rows_of
+        return order, first_row, pl.multiple_of(lax.rem(u, tiles) * wide, wide)
 
     def axes_of(order):
         a, b, c = order, lax.rem(order + 1, 3), lax.rem(order + 2, 3)
@@ -233,9 +252,8 @@
         pu, pd = step(pa, 1), step(pa, 3)
         lo, hi = pl.ds(0, 2), pl.ds(2, 2)
         drain(r1.at[u], rs_one.at[u])
-        f32 = jnp.float32
-        s1[u, pu, lo] = (s1[u, pu, lo].astype(f32) + r1[u, 0].astype(f32)).astype(jnp.bfloat16)
-        s1[u, pd, hi] = (s1[u, pd, hi].astype(f32) + r1[u, 1].astype(f32)).astype(jnp.bfloat16)
+        s1[u, pu, lo] += r1[u, 0]
+        s1[u, pd, hi] += r1[u, 1]
         remote(s1.at[u, pu, lo], r2.at[u, 0, lo], rs_send.at[2], rs_two.at[u], along(a, 1)).start()
         remote(s1.at[u, pd, hi], r2.at[u, 1, hi], rs_send.at[2], rs_two.at[u], along(a, 3)).start()
 
@@ -265,7 +283,9 @@
         drain(r4.at[u], rs_four.at[u])
         f32 = jnp.float32
         value = t2[u, pc].astype(f32) + r4[u, 0].astype(f32) + r4[u, 1].astype(f32) + r4[u, 2].astype(f32)
-        total[pl.ds(pl.multiple_of(lax.div(u, tiles) * half, half), half), pl.ds(column, lane)] = value
+        rows = pl.ds(pl.multiple_of(lax.div(u, tiles) * rows_of, rows_of), rows_of)
+        total[rows, pl.ds(column, lane)] = value[:rows_of]
+        total[rows, pl.ds(column + lane, lane)] = value[rows_of:]
 
         @pl.when(lax.rem(u, tiles) == tiles - 1)
         def _():
@@ -274,25 +294,18 @@
     owner = inner * 32 + outer
 
     def update(h):
-        rows = pl.ds(pl.multiple_of(h * half, half), half)
-        lows, highs = [], []
-        for g in range(width // group):
-            value = total[rows, g * group : (g + 1) * group]
-            high = jnp.floor(value * (1.0 / 128.0) + 0.5)
-            highs.append(high.astype(jnp.bfloat16))
-            lows.append((value - high * 128.0).astype(jnp.bfloat16))
-        stacked = jnp.concatenate(highs + lows, axis=0)
+        rows = pl.ds(pl.multiple_of(h * rows_of, rows_of), rows_of)
+        value = jnp.concatenate([total[rows, g * group : (g + 1) * group] for g in range(width // group)], axis=0)
+        high = jnp.floor(value * (1.0 / 128.0) + 0.5)
+        stacked = jnp.concatenate([high, value - high * 128.0], axis=0).astype(jnp.bfloat16)
         product = jnp.dot(stacked, table[...], preferred_element_type=jnp.float32)
-        parts = []
-        for g in range(width // group):
-            parts.append(
-                product[g * half : (g + 1) * half] * 128.0 + product[(g + 4) * half : (g + 5) * half]
-            )
+        product = product[: 4 * rows_of] * 128.0 + product[4 * rows_of :]
+        parts = [product[g * rows_of : (g + 1) * rows_of] for g in range(width // group)]
         for g, turned in enumerate(butterfly(parts)):
             columns = slice(g * group, (g + 1) * group)
-            offset = (owner * shard + h * half) * jnp.int32(wrap(width * hash_one)) + jnp.int32(wrap(g * group * hash_one))
+            offset = (owner * shard + h * rows_of) * jnp.int32(wrap(width * hash_one)) + jnp.int32(wrap(g * group * hash_one))
             mean = turned * decode
-            mean = jnp.where(negative(base[:half] + offset), -mean, mean)
+            mean = jnp.where(negative(base[...] + offset), -mean, mean)
             one = beta_one * adam_in[1, rows, columns] + (1.0 - beta_one) * mean
             two = beta_two * adam_in[2, rows, columns] + (1.0 - beta_two) * mean * mean
             old = adam_in[0, rows, columns]
@@ -301,28 +314,28 @@
             fresh[1, rows, columns] = one
             fresh[2, rows, columns] = two
             fresh[0, rows, columns] = new
-            param = new.astype(jnp.bfloat16)
-            for n in range(group // lane):
-                u = h * tiles + g * (group // lane) + n
-                order, _, _ = place(u, core)
-                _, _, c, pa, pb, pc = axes_of(order)
-                gath[u, pa, pb, pc] = param[:, n * lane : (n + 1) * lane]
-                for d in (1, 3, 2):
-                    remote(gath.at[u, pa, pb, pc], gath.at[u, pa, pb, pc], ag_send.at[0], ag_one.at[u], along(c, d)).start()
+            u = h * tiles + g
+            order, _, _ = place(u, core)
+            _, _, c, pa, pb, pc = axes_of(order)
+            mine = pa * 16 + pb * 4 + pc
+            gath[u, mine] = fold(new).astype(jnp.bfloat16)
+            for d in (1, 3, 2):
+                remote(gath.at[u, mine], gath.at[u, mine], ag_send.at[0], ag_one.at[u], along(c, d)).start()
 
     def ag1(u):
         order, _, _ = place(u, core)
         _, b, _, pa, pb, _ = axes_of(order)
         drain(r4.at[u], ag_one.at[u])
+        row = gath.at[u, pl.ds(pa * 16 + pb * 4, 4)]
         for d in (1, 3, 2):
-            remote(gath.at[u, pa, pb], gath.at[u, pa, pb], ag_send.at[1], ag_two.at[u], along(b, d)).start()
+            remote(row, row, ag_send.at[1], ag_two.at[u], along(b, d)).start()
 
     def ag2(u):
         order, _, _ = place(u, core)
         a, _, _, pa, _, _ = axes_of(order)
         drain(r3.at[u], ag_two.at[u])
         up, down = along(a, 1), along(a, 3)
-        lo, hi = gath.at[u, pa, pl.ds(0, 2)], gath.at[u, pa, pl.ds(2, 2)]
+        lo, hi = gath.at[u, pl.ds(pa * 16, 8)], gath.at[u, pl.ds(pa * 16 + 8, 8)]
         remote(lo, lo, ag_send.at[2], ag_near.at[u], up).start()
         remote(hi, hi, ag_send.at[2], ag_near.at[u], down).start()
         remote(hi, hi, ag_send.at[2], ag_far.at[u], up).start()
@@ -332,26 +345,52 @@
         order, _, _ = place(u, core)
         a, _, _, pa, _, _ = axes_of(order)
         drain(r1.at[u], ag_near.at[u])
-        lo, hi = gath.at[u, step(pa, 3), pl.ds(0, 2)], gath.at[u, step(pa, 1), pl.ds(2, 2)]
+        lo, hi = gath.at[u, pl.ds(step(pa, 3) * 16, 8)], gath.at[u, pl.ds(step(pa, 1) * 16 + 8, 8)]
         remote(lo, lo, ag_send.at[3], ag_far.at[u], along(a, 1)).start()
         remote(hi, hi, ag_send.at[3], ag_far.at[u], along(a, 3)).start()
 
+    def strides(order):
+        return pick(order, 16, 1, 4), pick(order, 4, 16, 1), pick(order, 1, 4, 16)
+
     def lay_out(u, source, from_core):
+        above = u - tiles
         order, first_row, column = place(u, from_core)
-
-        def work(i, j, k, row):
-            out[pl.ds(pl.multiple_of(row, half), half), pl.ds(column, lane)] = source[u, i, j, k]
-
-        each_tile(order, first_row, work)
+        first_row = first_row - rows_of
+        su, sa = strides(order), strides(place(above, from_core)[0])
+
+        def body(yy, carry):
+            row = first_row + row_of(1, yy)
+            at_u, at_a = yy * su[1], yy * sa[1]
+            for zz in range(4):
+                for xx in range(4):
+                    low = source[u, at_u + xx * su[0] + zz * su[2]].astype(jnp.float32)
+                    top = source[above, at_a + xx * sa[0] + zz * sa[2]].astype(jnp.float32)
+                    rows = pl.ds(pl.multiple_of(row + xx * shard + zz * 256, half), half)
+                    for n in range(2):
+                        part = slice(n * rows_of, (n + 1) * rows_of)
+                        both = jnp.concatenate([top[part], low[part]], axis=0)
+                        out[rows, pl.ds(column + n * lane, lane)] = both.astype(jnp.bfloat16)
+            return carry
+
+        lax.fori_loop(0, 4, body, 0)
+
+    def is_lower(u):
+        return lax.rem(lax.div(u, tiles), 2) == 1
 
     def ag4(u):
         drain(r2.at[u], ag_far.at[u])
         remote(gath.at[u], gath_other.at[u], ag_send.at[4], ag_core.at[u], twin).start()
-        lay_out(u, gath, core)
+
+        @pl.when(is_lower(u))
+        def _():
+            lay_out(u, gath, core)
 
     def ag5(u):
         drain(gath_other.at[u], ag_core.at[u])
-        lay_out(u, gath_other, 1 - core)
+
+        @pl.when(is_lower(u))
+        def _():
+            lay_out(u, gath_other, 1 - core)
 
     for copy in adam_copies:
         copy.wait()
@@ -384,6 +423,19 @@
     drain(gath, ag_send.at[4])
 
 
+def write_back(params, fresh, out, new_master, new_first, new_second, sems):
+    parts = 1
+    span = blocks // parts
+    copies = [pltpu.make_async_copy(fresh.at[n], ref, sems.at[n]) for n, ref in enumerate((new_master, new_first, new_second))]
+    for n in range(parts):
+        rows = pl.ds(n * span, span)
+        copies.append(pltpu.make_async_copy(params.at[rows], out.at[rows], sems.at[3 + n]))
+    for copy in copies:
+        copy.start()
+    for copy in copies:
+        copy.wait()
+
+
 def per_device(gradients, master, first_moment, second_moment):
     bf16, f32 = jnp.bfloat16, jnp.float32
     anywhere = pl.BlockSpec(memory_space=pl.ANY)
@@ -396,11 +448,12 @@
             pltpu.VMEM((blocks, width), bf16),
             pltpu.VMEM((3, shard, width), f32),
         ),
-        in_specs=[anywhere] * 4,
+        in_specs=[anywhere] * 5,
         out_specs=(in_vmem,) * 2,
         scratch_shapes=[
             pltpu.VMEM((blocks, width), f32),
-            pltpu.VMEM((sub, group), jnp.int32),
+            pltpu.VMEM((rows_of, group), jnp.int32),
+            pltpu.VMEM((blocks // 256, 8, width), jnp.int32),
             pltpu.VMEM((group, group), bf16),
             pltpu.VMEM((8, group), f32),
             pltpu.VMEM((8, 8, lane), f32),
@@ -416,9 +469,9 @@
             pltpu.VMEM((units, 3) + piece, bf16),
             pltpu.VMEM((units,) + piece, bf16),
             pltpu.VMEM((units, 3, half, lane), bf16),
-            pltpu.VMEM((units, 4, 4) + piece, bf16),
-            pltpu.VMEM((units, 4, 4) + piece, bf16),
-            dma((chunks,)), dma((3,)), dma((2,)), dma((2,)),
+            pltpu.VMEM((units, 64, half, lane), bf16),
+            pltpu.VMEM((units, 64, half, lane), bf16),
+            dma((chunks,)), dma((1,)), dma((3,)), dma((2,)), dma((2,)),
             dma((5,)), dma((units,)), dma((units,)), dma((units,)), dma((units,)), dma((units,)),
             dma((5,)), dma((units,)), dma((units,)), dma((units,)), dma((units,)), dma((units,)),
         ],
@@ -427,8 +480,22 @@
         ),
         cost_estimate=pl.CostEstimate(flops=2 * 2**32, bytes_accessed=2**25, transcendentals=0),
         name="reduce_step",
-    )(gradients, master, first_moment, second_moment)
-    return (fresh[0], fresh[1], fresh[2], params)
+    )(gradients, master, first_moment, second_moment, jnp.asarray(sign_words()))
+    params, new_master, new_first, new_second = pl.pallas_call(
+        write_back,
+        out_shape=(
+            jax.ShapeDtypeStruct((blocks, width), bf16),
+            jax.ShapeDtypeStruct((shard, width), f32),
+            jax.ShapeDtypeStruct((shard, width), f32),
+            jax.ShapeDtypeStruct((shard, width), f32),
+        ),
+        in_specs=[in_vmem] * 2,
+        out_specs=(anywhere,) * 4,
+        scratch_shapes=[dma((1 + 3,))],
+        compiler_params=pltpu.CompilerParams(vmem_limit_bytes=2**20),
+        name="write_back",
+    )(params, fresh)
+    return (new_master, new_first, new_second, params)
 
 
 def solution(mesh):

time: 81.2 us -> 78 us (0.961)
  local copies, waits for them, and re-layouts: 4.15 us -> 0 us
    pallas_call x0 -> x1, Pallas kernels: none -> 3.56 us  [per_device(): pl.pallas_call(write_back, out_shape=(jax.ShapeDtypeStruct((blocks, width...]
    unnamed x1 -> x0, local copies, waits for them, and re-layouts: 3.4 us -> none
    pallas_call x1, Pallas kernels: 76.3 us -> 73.4 us  [per_device(): pl.pallas_call(kernel, out_shape=(pltpu.VMEM((blocks, width), bf16), pltp...]
where the time goes in v3:
time: 78 us; the launch traced here: 77.6 us
  Pallas kernels  77 us (99%)
    pallas_call x1, Pallas kernels, per_device(): pl.pallas_call(kernel, out_shape=(pltpu.VMEM((blocks, width), bf16), pltp...  73.4 us
    pallas_call x1, Pallas kernels, per_device(): pl.pallas_call(write_back, out_shape=(jax.ShapeDtypeStruct((blocks, width...  3.56 us

profile of v3, /device:TPU:1, one launch (start us, length us, event | category | flops | bytes accessed | tf_op | source)
XLA Modules:
  0.0 77.6 jit_solution(4824829577446297338)
XLA Ops:
  0.6 73.4 %reduce_step.1 = (bf16[4096,1024]{1,0:T(8,128)(2,1)S(1)}, f32[3,32,1024]{2,1,0:T(8,128)S(1)}) custom-call(bf16[1,4096,1024]{2,1,0:T(8,128)(2,1)} %grad.1, f32[32,1024]{1,0:T(8,128)} %master.1, f32[32,1024]{1,0:T(8,128)} %first.1, f32[32,1024]{1,0:T(8,128)} %second.1, s32[16,8,1024]{2,1,0:T(8,128)} %constant.2.clone.words), custom_call_target="tpu_custom_call" | custom-call | flops 8589934592 | bytes 33554432 | tf_op jit(solution)/shard_map/reduce_step/pallas_call | solution.py:445
  74.1 3.6 %write_back.1 = (bf16[4096,1024]{1,0:T(8,128)(2,1)}, f32[32,1024]{1,0:T(8,128)}, f32[32,1024]{1,0:T(8,128)}, f32[32,1024]{1,0:T(8,128)}) custom-call(bf16[4096,1024]{1,0:T(8,128)(2,1)S(1)} %get-tuple-element.10.params, f32[3,32,1024]{2,1,0:T(8,128)S(1)} %get-tuple-element.11.fresh), custom_call_target="tpu_custom_call" | custom-call | tf_op jit(solution)/shard_map/write_back/pallas_call | solution.py:484

commit v4 on v3

--- a/solution.py
+++ b/solution.py
@@ -43,8 +43,8 @@
     return value - (1 << 32) if value & 0x80000000 else value
 
 
-RS = (0, 9, 14, 18, 24, 30)
-AG = (0, 4, 10, 15, 20, 23)
+RS = (0, 0, 7, 14, 21, 28)
+AG = (0, 5, 12, 18, 24, 27)
 
 
 def sign_words():
@@ -239,12 +239,10 @@
         each_tile(order, first_row, work)
         a, _, _, pa, _, _ = axes_of(order)
         up, down = along(a, 1), along(a, 3)
-        far, pu, pd = step(pa, 2), step(pa, 1), step(pa, 3)
+        far = step(pa, 2)
         lo, hi = pl.ds(0, 2), pl.ds(2, 2)
         remote(s1.at[u, far, lo], r1.at[u, 0], rs_send.at[1], rs_one.at[u], up).start()
         remote(s1.at[u, far, hi], r1.at[u, 1], rs_send.at[1], rs_one.at[u], down).start()
-        remote(s1.at[u, pu, hi], r2.at[u, 0, hi], rs_send.at[1], rs_two.at[u], up).start()
-        remote(s1.at[u, pd, lo], r2.at[u, 1, lo], rs_send.at[1], rs_two.at[u], down).start()
 
     def rs2(u):
         order, _, _ = place(u, core)
@@ -254,8 +252,8 @@
         drain(r1.at[u], rs_one.at[u])
         s1[u, pu, lo] += r1[u, 0]
         s1[u, pd, hi] += r1[u, 1]
-        remote(s1.at[u, pu, lo], r2.at[u, 0, lo], rs_send.at[2], rs_two.at[u], along(a, 1)).start()
-        remote(s1.at[u, pd, hi], r2.at[u, 1, hi], rs_send.at[2], rs_two.at[u], along(a, 3)).start()
+        remote(s1.at[u, pu], r2.at[u, 0], rs_send.at[2], rs_two.at[u], along(a, 1)).start()
+        remote(s1.at[u, pd], r2.at[u, 1], rs_send.at[2], rs_two.at[u], along(a, 3)).start()
 
     def rs3(u):
         order, _, _ = place(u, core)
@@ -338,16 +336,18 @@
         lo, hi = gath.at[u, pl.ds(pa * 16, 8)], gath.at[u, pl.ds(pa * 16 + 8, 8)]
         remote(lo, lo, ag_send.at[2], ag_near.at[u], up).start()
         remote(hi, hi, ag_send.at[2], ag_near.at[u], down).start()
-        remote(hi, hi, ag_send.at[2], ag_far.at[u], up).start()
-        remote(lo, lo, ag_send.at[2], ag_far.at[u], down).start()
 
     def ag3(u):
         order, _, _ = place(u, core)
         a, _, _, pa, _, _ = axes_of(order)
         drain(r1.at[u], ag_near.at[u])
         lo, hi = gath.at[u, pl.ds(step(pa, 3) * 16, 8)], gath.at[u, pl.ds(step(pa, 1) * 16 + 8, 8)]
-        remote(lo, lo, ag_send.at[3], ag_far.at[u], along(a, 1)).start()
-        remote(hi, hi, ag_send.at[3], ag_far.at[u], along(a, 3)).start()
+        up, down = along(a, 1), along(a, 3)
+        remote(lo, lo, ag_send.at[3], ag_far.at[u], up).start()
+        remote(hi, hi, ag_send.at[3], ag_far.at[u], down).start()
+        lo, hi = gath.at[u, pl.ds(pa * 16, 8)], gath.at[u, pl.ds(pa * 16 + 8, 8)]
+        remote(hi, hi, ag_send.at[3], ag_far.at[u], up).start()
+        remote(lo, lo, ag_send.at[3], ag_far.at[u], down).start()
 
     def strides(order):
         return pick(order, 16, 1, 4), pick(order, 4, 16, 1), pick(order, 1, 4, 16)
@@ -395,31 +395,37 @@
     for copy in adam_copies:
         copy.wait()
     lead = tiles - 1 + RS[5]
-    plan = [(ag5, lead + AG[5]), (ag4, lead + AG[4]), (ag3, lead + AG[3]), (ag2, lead + AG[2]), (ag1, lead + AG[1])]
-    plan += [(rs5, RS[5]), (rs4, RS[4]), (rs3, RS[3]), (rs2, RS[2]), (rs1, RS[1]), (rs0, RS[0])]
-
-    plan = plan[::-1]
-
-    def tick(t, carry):
-        for work, delay in plan:
-            @pl.when(jnp.logical_and(t >= delay, t < delay + units))
-            def _(work=work, delay=delay):
+    plan = [(rs1, RS[1]), (rs2, RS[2]), (rs3, RS[3]), (rs4, RS[4]), (rs5, RS[5])]
+    plan += [(ag1, lead + AG[1]), (ag2, lead + AG[2]), (ag3, lead + AG[3]), (ag4, lead + AG[4]), (ag5, lead + AG[5])]
+
+    def first_step(u, carry):
+        rs0(u)
+        return carry
+
+    lax.fori_loop(0, units, first_step, 0)
+
+    marks = sorted({delay for _, delay in plan} | {delay + units for _, delay in plan})
+    for begin, end in zip(marks, marks[1:]):
+        running = [(work, delay) for work, delay in plan if delay <= begin and end <= delay + units]
+
+        def tick(t, carry, running=running):
+            for work, delay in running:
                 work(t - delay)
-        return carry
-
-    lax.fori_loop(0, units + lead + AG[5], tick, 0)
+            return carry
+
+        lax.fori_loop(begin, end, tick, 0)
 
     for n, box in enumerate((peaks_one, peaks_two)):
         drain(box.at[pl.ds(1, (7, 15)[n]), :1], peak_send.at[n])
     drain(other, rs_send.at[0])
-    drain(r2, rs_send.at[1])
-    drain(r1, rs_send.at[2])
+    drain(r1, rs_send.at[1])
+    drain(r2, rs_send.at[2])
     drain(r3, rs_send.at[3])
     drain(r4, rs_send.at[4])
     drain(r4, ag_send.at[0])
     drain(r3, ag_send.at[1])
-    drain(r2, ag_send.at[2])
-    drain(r1, ag_send.at[3])
+    drain(r1, ag_send.at[2])
+    drain(r2, ag_send.at[3])
     drain(gath, ag_send.at[4])
 
 

time: 78 us -> 75.2 us (0.964)
  Pallas kernels: 77 us -> 74.4 us
    pallas_call x1, Pallas kernels: 73.4 us -> 70.9 us  [per_device(): pl.pallas_call(kernel, out_shape=(pltpu.VMEM((blocks, width), bf16), pltp...]
where the time goes in v4:
time: 75.2 us; the launch traced here: 75.1 us
  Pallas kernels  74.4 us (99%)
    pallas_call x1, Pallas kernels, per_device(): pl.pallas_call(kernel, out_shape=(pltpu.VMEM((blocks, width), bf16), pltp...  70.9 us
    pallas_call x1, Pallas kernels, per_device(): pl.pallas_call(write_back, out_shape=(jax.ShapeDtypeStruct((blocks, width...  3.56 us

profile of v4, /device:TPU:1, one launch (start us, length us, event | category | flops | bytes accessed | tf_op | source)
XLA Modules:
  0.0 75.1 jit_solution(3383566548902536502)
XLA Ops:
  0.6 70.9 %reduce_step.1 = (bf16[4096,1024]{1,0:T(8,128)(2,1)S(1)}, f32[3,32,1024]{2,1,0:T(8,128)S(1)}) custom-call(bf16[1,4096,1024]{2,1,0:T(8,128)(2,1)} %grad.1, f32[32,1024]{1,0:T(8,128)} %master.1, f32[32,1024]{1,0:T(8,128)} %first.1, f32[32,1024]{1,0:T(8,128)} %second.1, s32[16,8,1024]{2,1,0:T(8,128)} %constant.2.clone.words), custom_call_target="tpu_custom_call" | custom-call | flops 8589934592 | bytes 33554432 | tf_op jit(solution)/shard_map/reduce_step/pallas_call | solution.py:451
  71.5 3.6 %write_back.1 = (bf16[4096,1024]{1,0:T(8,128)(2,1)}, f32[32,1024]{1,0:T(8,128)}, f32[32,1024]{1,0:T(8,128)}, f32[32,1024]{1,0:T(8,128)}) custom-call(bf16[4096,1024]{1,0:T(8,128)(2,1)S(1)} %get-tuple-element.10.params, f32[3,32,1024]{2,1,0:T(8,128)S(1)} %get-tuple-element.11.fresh), custom_call_target="tpu_custom_call" | custom-call | tf_op jit(solution)/shard_map/write_back/pallas_call | solution.py:490

commit v5 on v4

--- a/solution.py
+++ b/solution.py
@@ -30,6 +30,7 @@
 wide = 2 * lane
 tiles = width // wide
 units = shard // rows_of * tiles
+early = tiles
 chunk = 512
 chunks = blocks // chunk
 sub = 512
@@ -43,8 +44,8 @@
     return value - (1 << 32) if value & 0x80000000 else value
 
 
-RS = (0, 0, 7, 14, 21, 28)
-AG = (0, 5, 12, 18, 24, 27)
+RS = (0, 0, 7, 14, 22, 29)
+AG = (0, 6, 13, 19, 26, 30)
 
 
 def sign_words():
@@ -70,18 +71,18 @@
     return jnp.where(order == 0, v0, jnp.where(order == 1, v1, v2))
 
 
-def row_of(axis, v):
+def shard_of(axis, v):
     if isinstance(v, int):
-        return pick(axis, v * shard, (v % 2) * 128 + (v // 2) * 2048, v * 256)
-    return pick(axis, v * shard, lax.rem(v, 2) * 128 + lax.div(v, 2) * 2048, v * 256)
+        return pick(axis, v, (v % 2) * 4 + (v // 2) * 64, v * 8)
+    return pick(axis, v, lax.rem(v, 2) * 4 + lax.div(v, 2) * 64, v * 8)
 
 
 def kernel(
     grad, master, first, second, words,
     out, fresh,
-    rot, base, signs, table, peak, peaks_one, peaks_two, adam_in, total,
+    rot, twin_rot, base, signs, table, peak, peaks_one, peaks_two, adam_in, total,
     other, core_in, s1, r1, r2, t1, r3, t2, r4, gath, gath_other,
-    grad_sem, sign_sem, adam_sem, peak_send, peak_recv,
+    grad_sem, sign_sem, twin_send, twin_recv, adam_sem, peak_send, peak_recv,
     rs_send, rs_core, rs_one, rs_two, rs_three, rs_four,
     ag_send, ag_one, ag_two, ag_near, ag_far, ag_core,
 ):
@@ -168,7 +169,8 @@
         pieces = [turned[g * sub : (g + 1) * sub] for g in range(width // group)]
         top = peak[...]
         for g, piece in enumerate(butterfly(pieces)):
-            rot[rows, g * group : (g + 1) * group] = piece
+            held = pl.ds(pl.multiple_of(i * (sub // shard), sub // shard), sub // shard)
+            rot[held, :, g * group : (g + 1) * group] = piece.reshape(sub // shard, shard, group)
             top = jnp.maximum(top, jnp.max(jnp.abs(piece).reshape(sub // 8, 8, group), axis=0))
         peak[...] = top
         return carry
@@ -177,10 +179,19 @@
 
     pl.semaphore_wait(barrier, len(partners))
     best = jnp.max(jnp.maximum(peak[:, :lane], peak[:, lane:]), axis=0, keepdims=True)
+    twin_copies = []
+    for n in range(2):
+        span = pl.ds(pl.multiple_of(n * 64 + (1 - core) * 32, 32), 32)
+        twin_copies.append(
+            remote(rot.at[span, pl.ds(0, rows_of)], twin_rot.at[span], twin_send.at[n], twin_recv.at[n], twin)
+        )
     for n, (stage, box) in enumerate(((column, peaks_one), (plane, peaks_two))):
         box[0, :1] = best
         for k, target in enumerate(stage):
             remote(box.at[0, :1], box.at[1 + k, :1], peak_send.at[n], peak_recv.at[n], target).start()
+        if n == 0:
+            for copy in twin_copies:
+                copy.start()
         arrived = box.at[pl.ds(1, len(stage)), :1]
         drain(arrived, peak_recv.at[n])
         for k in range(len(stage)):
@@ -192,8 +203,12 @@
     def fold(value):
         return jnp.concatenate([value[:, :lane], value[:, lane:]], axis=0)
 
-    def quantise(row, column):
-        value = rot[pl.ds(pl.multiple_of(row, rows_of), rows_of), pl.ds(column, wide)]
+    def quantise(owned, row, column):
+        value = rot[owned, pl.ds(row, rows_of), pl.ds(column, wide)]
+        return fold(jnp.floor(value * ratio + 0.5))
+
+    def quantise_twin(owned, column):
+        value = twin_rot[owned, :, pl.ds(column, wide)]
         return fold(jnp.floor(value * ratio + 0.5))
 
     def place(u, owner):
@@ -205,13 +220,13 @@
         a, b, c = order, lax.rem(order + 1, 3), lax.rem(order + 2, 3)
         return a, b, c, pick(a, x, y, z), pick(b, x, y, z), pick(c, x, y, z)
 
-    def each_tile(order, first_row, work):
+    def each_tile(order, first, work):
         a, b, c = order, lax.rem(order + 1, 3), lax.rem(order + 2, 3)
-        in_b = [row_of(b, j) for j in range(4)]
-        in_c = [row_of(c, k) for k in range(4)]
+        in_b = [shard_of(b, j) for j in range(4)]
+        in_c = [shard_of(c, k) for k in range(4)]
 
         def body(i, carry):
-            start = first_row + row_of(a, i)
+            start = first + shard_of(a, i)
             for j in range(4):
                 for k in range(4):
                     work(i, j, k, start + in_b[j] + in_c[k])
@@ -219,24 +234,42 @@
 
         lax.fori_loop(0, 4, body, 0)
 
+    def row_in(u):
+        return pl.multiple_of(lax.div(u, tiles) * rows_of, rows_of)
+
     def rs0(u):
-        order, first_row, column = place(u, 1 - core)
-
-        def work(i, j, k, row):
-            other[u, i, j, k] = quantise(row, column).astype(jnp.bfloat16)
-
-        each_tile(order, first_row, work)
+        order, _, column = place(u, 1 - core)
+        row = row_in(u)
+
+        def work(i, j, k, owned):
+            other[u, i, j, k] = quantise(owned, row, column).astype(jnp.bfloat16)
+
+        each_tile(order, 32 * (1 - core), work)
         remote(other.at[u], core_in.at[u], rs_send.at[0], rs_core.at[u], twin).start()
 
+    def rs1_early(u):
+        order, _, column = place(u, core)
+        row = row_in(u)
+
+        def work(i, j, k, owned):
+            s1[u, i, j, k] = (quantise(owned, row, column) + quantise_twin(owned, column)).astype(jnp.bfloat16)
+
+        each_tile(order, 32 * core, work)
+        send_far(u, order)
+
     def rs1(u):
-        order, first_row, column = place(u, core)
+        order, _, column = place(u, core)
+        row = row_in(u)
         drain(core_in.at[u], rs_core.at[u])
 
-        def work(i, j, k, row):
-            mine = quantise(row, column)
+        def work(i, j, k, owned):
+            mine = quantise(owned, row, column)
             s1[u, i, j, k] = (mine + core_in[u, i, j, k].astype(jnp.float32)).astype(jnp.bfloat16)
 
-        each_tile(order, first_row, work)
+        each_tile(order, 32 * core, work)
+        send_far(u, order)
+
+    def send_far(u, order):
         a, _, _, pa, _, _ = axes_of(order)
         up, down = along(a, 1), along(a, 3)
         far = step(pa, 2)
@@ -359,7 +392,7 @@
         su, sa = strides(order), strides(place(above, from_core)[0])
 
         def body(yy, carry):
-            row = first_row + row_of(1, yy)
+            row = first_row + shard_of(1, yy) * shard
             at_u, at_a = yy * su[1], yy * sa[1]
             for zz in range(4):
                 for xx in range(4):
@@ -395,29 +428,36 @@
     for copy in adam_copies:
         copy.wait()
     lead = tiles - 1 + RS[5]
-    plan = [(rs1, RS[1]), (rs2, RS[2]), (rs3, RS[3]), (rs4, RS[4]), (rs5, RS[5])]
-    plan += [(ag1, lead + AG[1]), (ag2, lead + AG[2]), (ag3, lead + AG[3]), (ag4, lead + AG[4]), (ag5, lead + AG[5])]
-
-    def first_step(u, carry):
-        rs0(u)
-        return carry
-
-    lax.fori_loop(0, units, first_step, 0)
-
-    marks = sorted({delay for _, delay in plan} | {delay + units for _, delay in plan})
+    plan = [(rs1, RS[1], early), (rs2, RS[2], 0), (rs3, RS[3], 0), (rs4, RS[4], 0), (rs5, RS[5], 0)]
+    plan += [(work, lead + AG[n + 1], 0) for n, work in enumerate((ag1, ag2, ag3, ag4, ag5))]
+    for copy in twin_copies:
+        copy.wait_recv()
+
+    def repeat(work, begin, end):
+        def body(u, carry):
+            work(u)
+            return carry
+
+        lax.fori_loop(begin, end, body, 0)
+
+    repeat(rs1_early, 0, early)
+    repeat(rs0, early, units)
+
+    marks = sorted({delay + first for _, delay, first in plan} | {delay + units for _, delay, _ in plan})
     for begin, end in zip(marks, marks[1:]):
-        running = [(work, delay) for work, delay in plan if delay <= begin and end <= delay + units]
-
-        def tick(t, carry, running=running):
+        running = [(work, delay) for work, delay, first in plan if delay + first <= begin and end <= delay + units]
+
+        def tick(t, running=running):
             for work, delay in running:
                 work(t - delay)
-            return carry
-
-        lax.fori_loop(begin, end, tick, 0)
-
+
+        repeat(tick, begin, end)
+
+    for copy in twin_copies:
+        copy.wait_send()
     for n, box in enumerate((peaks_one, peaks_two)):
         drain(box.at[pl.ds(1, (7, 15)[n]), :1], peak_send.at[n])
-    drain(other, rs_send.at[0])
+    drain(other.at[pl.ds(early, units - early)], rs_send.at[0])
     drain(r1, rs_send.at[1])
     drain(r2, rs_send.at[2])
     drain(r3, rs_send.at[3])
@@ -457,7 +497,8 @@
         in_specs=[anywhere] * 5,
         out_specs=(in_vmem,) * 2,
         scratch_shapes=[
-            pltpu.VMEM((blocks, width), f32),
+            pltpu.VMEM((blocks // shard, shard, width), f32),
+            pltpu.VMEM((blocks // shard, rows_of, width), f32),
             pltpu.VMEM((rows_of, group), jnp.int32),
             pltpu.VMEM((blocks // 256, 8, width), jnp.int32),
             pltpu.VMEM((group, group), bf16),
@@ -477,7 +518,7 @@
             pltpu.VMEM((units, 3, half, lane), bf16),
             pltpu.VMEM((units, 64, half, lane), bf16),
             pltpu.VMEM((units, 64, half, lane), bf16),
-            dma((chunks,)), dma((1,)), dma((3,)), dma((2,)), dma((2,)),
+            dma((chunks,)), dma((1,)), dma((2,)), dma((2,)), dma((3,)), dma((2,)), dma((2,)),
             dma((5,)), dma((units,)), dma((units,)), dma((units,)), dma((units,)), dma((units,)),
             dma((5,)), dma((units,)), dma((units,)), dma((units,)), dma((units,)), dma((units,)),
         ],

time: 75.2 us -> 73.5 us (0.977)
  Pallas kernels: 74.4 us -> 72.7 us
    pallas_call x1, Pallas kernels: 70.9 us -> 69.2 us  [per_device(): pl.pallas_call(kernel, out_shape=(pltpu.VMEM((blocks, width), bf16), pltp...]
where the time goes in v5:
time: 73.5 us; the launch traced here: 73.4 us
  Pallas kernels  72.7 us (99%)
    pallas_call x1, Pallas kernels, per_device(): pl.pallas_call(kernel, out_shape=(pltpu.VMEM((blocks, width), bf16), pltp...  69.2 us
    pallas_call x1, Pallas kernels, per_device(): pl.pallas_call(write_back, out_shape=(jax.ShapeDtypeStruct((blocks, width...  3.56 us

profile of v5, /device:TPU:1, one launch (start us, length us, event | category | flops | bytes accessed | tf_op | source)
XLA Modules:
  0.0 73.4 jit_solution(1785231468851075238)
XLA Ops:
  0.6 69.2 %reduce_step.1 = (bf16[4096,1024]{1,0:T(8,128)(2,1)S(1)}, f32[3,32,1024]{2,1,0:T(8,128)S(1)}) custom-call(bf16[1,4096,1024]{2,1,0:T(8,128)(2,1)} %grad.1, f32[32,1024]{1,0:T(8,128)} %master.1, f32[32,1024]{1,0:T(8,128)} %first.1, f32[32,1024]{1,0:T(8,128)} %second.1, s32[16,8,1024]{2,1,0:T(8,128)} %constant.2.clone.words), custom_call_target="tpu_custom_call" | custom-call | flops 8589934592 | bytes 33554432 | tf_op jit(solution)/shard_map/reduce_step/pallas_call | solution.py:491
  69.8 3.6 %write_back.1 = (bf16[4096,1024]{1,0:T(8,128)(2,1)}, f32[32,1024]{1,0:T(8,128)}, f32[32,1024]{1,0:T(8,128)}, f32[32,1024]{1,0:T(8,128)}) custom-call(bf16[4096,1024]{1,0:T(8,128)(2,1)S(1)} %get-tuple-element.10.params, f32[3,32,1024]{2,1,0:T(8,128)S(1)} %get-tuple-element.11.fresh), custom_call_target="tpu_custom_call" | custom-call | tf_op jit(solution)/shard_map/write_back/pallas_call | solution.py:531

commit v6 on v5

--- a/solution.py
+++ b/solution.py
@@ -393,16 +393,17 @@
 
         def body(yy, carry):
             row = first_row + shard_of(1, yy) * shard
+            view = out.at[pl.ds(pl.multiple_of(row, half), 880), pl.ds(column, wide)]
             at_u, at_a = yy * su[1], yy * sa[1]
             for zz in range(4):
                 for xx in range(4):
                     low = source[u, at_u + xx * su[0] + zz * su[2]].astype(jnp.float32)
                     top = source[above, at_a + xx * sa[0] + zz * sa[2]].astype(jnp.float32)
-                    rows = pl.ds(pl.multiple_of(row + xx * shard + zz * 256, half), half)
+                    first = xx * shard + zz * 256
                     for n in range(2):
                         part = slice(n * rows_of, (n + 1) * rows_of)
                         both = jnp.concatenate([top[part], low[part]], axis=0)
-                        out[rows, pl.ds(column + n * lane, lane)] = both.astype(jnp.bfloat16)
+                        view[first : first + half, n * lane : (n + 1) * lane] = both.astype(jnp.bfloat16)
             return carry
 
         lax.fori_loop(0, 4, body, 0)

time: 73.5 us -> 72.7 us (0.989)
    pallas_call x1, Pallas kernels: 69.2 us -> 68.4 us  [per_device(): pl.pallas_call(kernel, out_shape=(pltpu.VMEM((blocks, width), bf16), pltp...]
where the time goes in v6:
time: 72.7 us; the launch traced here: 72.6 us
  Pallas kernels  72 us (99%)
    pallas_call x1, Pallas kernels, per_device(): pl.pallas_call(kernel, out_shape=(pltpu.VMEM((blocks, width), bf16), pltp...  68.4 us
    pallas_call x1, Pallas kernels, per_device(): pl.pallas_call(write_back, out_shape=(jax.ShapeDtypeStruct((blocks, width...  3.56 us

profile of v6, /device:TPU:1, one launch (start us, length us, event | category | flops | bytes accessed | tf_op | source)
XLA Modules:
  0.0 72.6 jit_solution(1264218488052733350)
XLA Ops:
  0.6 68.4 %reduce_step.1 = (bf16[4096,1024]{1,0:T(8,128)(2,1)S(1)}, f32[3,32,1024]{2,1,0:T(8,128)S(1)}) custom-call(bf16[1,4096,1024]{2,1,0:T(8,128)(2,1)} %grad.1, f32[32,1024]{1,0:T(8,128)} %master.1, f32[32,1024]{1,0:T(8,128)} %first.1, f32[32,1024]{1,0:T(8,128)} %second.1, s32[16,8,1024]{2,1,0:T(8,128)} %constant.2.clone.words), custom_call_target="tpu_custom_call" | custom-call | flops 8589934592 | bytes 33554432 | tf_op jit(solution)/shard_map/reduce_step/pallas_call | solution.py:492
  69.1 3.6 %write_back.1 = (bf16[4096,1024]{1,0:T(8,128)(2,1)}, f32[32,1024]{1,0:T(8,128)}, f32[32,1024]{1,0:T(8,128)}, f32[32,1024]{1,0:T(8,128)}) custom-call(bf16[4096,1024]{1,0:T(8,128)(2,1)S(1)} %get-tuple-element.10.params, f32[3,32,1024]{2,1,0:T(8,128)S(1)} %get-tuple-element.11.fresh), custom_call_target="tpu_custom_call" | custom-call | tf_op jit(solution)/shard_map/write_back/pallas_call | solution.py:532

commit v7 on v6

--- a/solution.py
+++ b/solution.py
@@ -406,7 +406,7 @@
                         view[first : first + half, n * lane : (n + 1) * lane] = both.astype(jnp.bfloat16)
             return carry
 
-        lax.fori_loop(0, 4, body, 0)
+        lax.fori_loop(0, 4, body, 0, unroll=True)
 
     def is_lower(u):
         return lax.rem(lax.div(u, tiles), 2) == 1

time: 72.7 us -> 72.7 us (level)
  no operation moved by 1% of the time
where the time goes in v7:
time: 72.7 us; the launch traced here: 72.6 us
  Pallas kernels  72 us (99%)
    pallas_call x1, Pallas kernels, per_device(): pl.pallas_call(kernel, out_shape=(pltpu.VMEM((blocks, width), bf16), pltp...  68.4 us
    pallas_call x1, Pallas kernels, per_device(): pl.pallas_call(write_back, out_shape=(jax.ShapeDtypeStruct((blocks, width...  3.56 us

profile of v7, /device:TPU:1, one launch (start us, length us, event | category | flops | bytes accessed | tf_op | source)
XLA Modules:
  0.0 72.6 jit_solution(10469651125323510371)
XLA Ops:
  0.6 68.4 %reduce_step.1 = (bf16[4096,1024]{1,0:T(8,128)(2,1)S(1)}, f32[3,32,1024]{2,1,0:T(8,128)S(1)}) custom-call(bf16[1,4096,1024]{2,1,0:T(8,128)(2,1)} %grad.1, f32[32,1024]{1,0:T(8,128)} %master.1, f32[32,1024]{1,0:T(8,128)} %first.1, f32[32,1024]{1,0:T(8,128)} %second.1, s32[16,8,1024]{2,1,0:T(8,128)} %constant.2.clone.words), custom_call_target="tpu_custom_call" | custom-call | flops 8589934592 | bytes 33554432 | tf_op jit(solution)/shard_map/reduce_step/pallas_call | solution.py:492
  69.0 3.6 %write_back.1 = (bf16[4096,1024]{1,0:T(8,128)(2,1)}, f32[32,1024]{1,0:T(8,128)}, f32[32,1024]{1,0:T(8,128)}, f32[32,1024]{1,0:T(8,128)}) custom-call(bf16[4096,1024]{1,0:T(8,128)(2,1)S(1)} %get-tuple-element.10.params, f32[3,32,1024]{2,1,0:T(8,128)S(1)} %get-tuple-element.11.fresh), custom_call_target="tpu_custom_call" | custom-call | tf_op jit(solution)/shard_map/write_back/pallas_call | solution.py:532
